TPU v7x, 512 devices: a whole 4x8x8 slice. The times are simulated.
512 devices in a mesh: clip: 32 (over x, y), seq: 16 (over z, core).
Axes of the slice: x: 4, y: 8, z: 8, core: 2. Of those that a mesh axis runs over, the one named last changes fastest.
Arguments:
- queries: bfloat16 [32, 2048, 4096], P('clip', 'seq'), may hold values from -34 to 34
- keys: bfloat16 [32, 2048, 4096], P('clip', 'seq'), may hold values from -6 to 6
- values: bfloat16 [32, 2048, 4096], P('clip', 'seq'), may hold values from -6 to 6
- frame_counts: int32 [128], P('clip'), may hold values from 1 to 4
- assignment: int32 [32], P('clip'), may hold values from 0 to 127
- timesteps: int32 [32], P('clip'), may hold values from 0 to 999
- gate_gain: float32 [4096], replicated, may hold values from -3 to 3
Outputs:
- attended: bfloat16 [32, 2048, 4096], P('clip', 'seq')
All inputs are finite; a program needn't handle non-finite values.
Results may differ from a plain program's by a relative error of at most 0.0086.
Values may be sent and summed in bfloat16 or wider, within the bound.
A program may use at most 128 MiB of HBM per device.

v0:
```python
import jax
import jax.numpy as jnp
from jax import lax
from jax.sharding import Mesh
from jax.sharding import PartitionSpec as P

HD = 128
FRAME_TOK = 448
GRID_W = 28
CLIP = ("clip_0", "clip_1")


def in_order(tiles, dim):
    dims = list(tiles.shape[1:])
    dims[dim] *= tiles.shape[0]
    return jnp.moveaxis(tiles, 0, dim).reshape(dims)


def all_blocks(shard, axes, sequence):
    tiles = shard
    for k in sequence:
        tiles = lax.all_gather(tiles, axes[k])
    done = sequence[::-1]
    back = [done.index(k) for k in range(len(axes))]
    tiles = tiles.transpose(*back, *range(len(axes), tiles.ndim))
    return tiles.reshape(-1, *shard.shape)


def gathered_by_axis(shard, axes, sequence, dim):
    return in_order(all_blocks(shard, axes, sequence), dim)


def sent_together(arrays, axis, split_dim, concat_dim, along):
    both = jnp.concatenate(arrays, axis=along)
    out, at, done = (
        lax.all_to_all(both, axis, split_axis=split_dim, concat_axis=concat_dim, tiled=True),
        0,
        [],
    )
    for a in arrays:
        done.append(lax.slice_in_dim(out, at, at + a.shape[along], axis=along))
        at += a.shape[along]
    return tuple(done)


def rope_tables(count):
    position = jnp.arange(count, dtype=jnp.int32)
    frame = (position // FRAME_TOK).astype(jnp.float32)
    within = position % FRAME_TOK
    row_pos = (within // GRID_W).astype(jnp.float32)
    col_pos = (within % GRID_W).astype(jnp.float32)
    temporal = jnp.arange(22, dtype=jnp.float32)
    spatial = jnp.arange(21, dtype=jnp.float32)
    inv_time = 10000.0 ** (-2.0 * temporal / 44.0)
    inv_space = 10000.0 ** (-2.0 * spatial / 42.0)
    angles = jnp.concatenate(
        [
            frame[:, None] * inv_time[None, :],
            row_pos[:, None] * inv_space[None, :],
            col_pos[:, None] * inv_space[None, :],
        ],
        axis=1,
    )
    return (jnp.cos(angles), jnp.sin(angles))


def rotate(vectors, cosine, sine):
    half = vectors.shape[-1] // 2
    first = vectors[..., :half].astype(jnp.float32)
    second = vectors[..., half:].astype(jnp.float32)
    cos_b = cosine[:, None, :]
    sin_b = sine[:, None, :]
    return jnp.concatenate(
        [first * cos_b - second * sin_b, first * sin_b + second * cos_b], axis=-1
    ).astype(jnp.bfloat16)


def masked_scores(q_block, key_rot, width, length, scale):
    scores = (
        jnp.einsum("qhd,khd->hqk", q_block, key_rot, preferred_element_type=jnp.float32) * scale
    )
    key_pos = jnp.arange(width, dtype=jnp.int32)
    return jnp.where(key_pos[None, None, :] < length, scores, -jnp.inf)


def attend(query_rot, key_rot, value, length):
    count = query_rot.shape[0]
    width = min(512, count)
    scale = HD ** (-0.5)
    results = []
    for start in range(0, count, width):
        q_block = query_rot[start : start + width]
        scores = masked_scores(q_block, key_rot, count, length, scale)
        top = jnp.max(scores, axis=-1, keepdims=True)
        weights = jnp.exp(scores - top)
        total = jnp.sum(weights, axis=-1)
        mixed = jnp.einsum(
            "hqk,khd->qhd", weights.astype(jnp.bfloat16), value, preferred_element_type=jnp.float32
        )
        results.append(mixed / jnp.transpose(total)[:, :, None])
    return jnp.concatenate(results, axis=0).astype(jnp.bfloat16)


def local(queries, keys, values, frame_counts, assignment, timesteps, gate_gain):
    counts_all = gathered_by_axis(frame_counts, CLIP, (0, 1), 0)
    slots = jnp.arange(counts_all.shape[0], dtype=jnp.int32)
    picked = jnp.sum(jnp.where(slots == assignment[0], counts_all, 0))
    length = picked * FRAME_TOK
    fraction = timesteps[0].astype(jnp.float32) / 1000.0
    sigma = 5.0 * fraction / (1.0 + 4.0 * fraction)
    tok_rows = queries.shape[1]
    feature_count = queries.shape[2]
    groups = lax.axis_size("seq")
    heads_local = feature_count // HD // groups
    query_rows = queries.reshape(tok_rows, groups, heads_local, HD)
    key_rows = keys.reshape(tok_rows, groups, heads_local, HD)
    value_rows = values.reshape(tok_rows, groups, heads_local, HD)
    q_heads, k_heads, v_heads = sent_together((query_rows, key_rows, value_rows), "seq", 1, 0, 2)
    count = q_heads.shape[0]
    heads_here = q_heads.shape[2]
    cosine, sine = rope_tables(count)
    query_rot = rotate(q_heads.reshape(count, heads_here, HD), cosine, sine)
    key_rot = rotate(k_heads.reshape(count, heads_here, HD), cosine, sine)
    mixed = attend(query_rot, key_rot, v_heads.reshape(count, heads_here, HD), length)
    mixed = mixed.reshape(count, 1, heads_here, HD)
    returned = lax.all_to_all(mixed, "seq", split_axis=0, concat_axis=1, tiled=True)
    returned = returned.reshape(tok_rows, feature_count).astype(jnp.float32)
    position = lax.axis_index("seq") * tok_rows + jnp.arange(tok_rows, dtype=jnp.int32)
    gated = returned * (1.0 + sigma * gate_gain[None, :])
    attended = jnp.where(position[:, None] < length, gated, 0.0).astype(jnp.bfloat16)
    return attended[None]


def solution(mesh):
    finer = Mesh(mesh.devices.reshape(4, 8, mesh.shape["seq"]), ("clip_0", "clip_1", "seq"))
    in_specs = (
        P(CLIP, "seq", None),
        P(CLIP, "seq", None),
        P(CLIP, "seq", None),
        P(CLIP),
        P(CLIP),
        P(CLIP),
        P(),
    )
    out_specs = P(CLIP, "seq", None)
    return jax.shard_map(local, mesh=finer, in_specs=in_specs, out_specs=out_specs, check_vma=False)
```

profile of v0, /device:TPU:1, one launch (start us, length us, event | category | flops | bytes accessed | tf_op | source)
XLA Modules:
  0.0 183.7 jit_solution(16581078526620594948)
XLA Ops:
  0.0 2.3 %copy.23 = bf16[1,128,4096]{1,2,0:T(8,128)(2,1)} copy(bf16[1,128,4096]{2,1,0:T(8,128)(2,1)} %param.7) | data formatting | bytes 2097152 | tf_op args[0]
  2.3 2.3 %copy.24 = bf16[1,128,4096]{1,2,0:T(8,128)(2,1)} copy(bf16[1,128,4096]{2,1,0:T(8,128)(2,1)} %param.8) | data formatting | bytes 2097152 | tf_op args[1]
  4.6 2.3 %copy.25 = bf16[1,128,4096]{1,2,0:T(8,128)(2,1)} copy(bf16[1,128,4096]{2,1,0:T(8,128)(2,1)} %param.9) | data formatting | bytes 2097152 | tf_op args[2]
  6.8 2.0 %pad_maximum_fusion = bf16[128,16,6,128]{0,3,2,1:T(8,128)(2,1)S(1)} fusion(bf16[128,16,2,128]{0,3,2,1:T(8,128)(2,1)} %bitcast.88, bf16[128,16,2,128]{0,3,2,1:T(8,128)(2,1)} %bitcast.87, bf16[128,16,2,128]{0,3,2,1:T(8,128)(2,1)} %bitcast.86), kind=kLoop, calls=%fused_computation.28 | loop fusion | flops 3145728 | bytes 6291456 | tf_op jit(solution)/shard_map/concatenate | solution.py:34
  8.9 2.8 %copy.26 = bf16[128,16,6,128]{3,0,2,1:T(8,128)(2,1)} copy(bf16[128,16,6,128]{0,3,2,1:T(8,128)(2,1)S(1)} %pad_maximum_fusion) | data formatting | bytes 6291456 | tf_op jit(solution)/shard_map/concatenate | solution.py:34
  11.7 11.8 %all-to-all-start = ((bf16[128,16,6,128]{3,0,2,1:T(8,128)(2,1)}), bf16[128,16,6,128]{3,0,2,1:T(8,128)(2,1)S(1)}, u32[]{:S(2)}, u32[]{:S(2)}) async-start(bf16[128,16,6,128]{3,0,2,1:T(8,128)(2,1)} %copy.26), calls=%async_computation | async-start | bytes 6291456 | tf_op jit(solution)/shard_map/all_to_all | solution.py:36
  23.5 1.3 dynamic-slice
  25.4 0.0 copy-done.9
  25.4 0.2 dynamic-update-slice
  25.7 7.4 %all-reduce = s32[16]{0:T(128)S(1)} all-reduce(s32[16]{0:T(128)S(1)} %dynamic-update-slice), channel_id=2, replica_groups=mesh['clip_0'=4,'clip_1'=8,'seq'=16] {'clip_0'}, use_global_device_ids=true, to_apply=%add | all-reduce | flops 16 | bytes 128
  33.1 0.1 reshape.313
  33.9 20.1 %all-gather.2 = s32[8,4,4]{2,1,0:T(4,128)S(1)} all-gather(s32[1,4,4]{2,1,0:T(4,128)S(1)} %reshape.313), channel_id=3, replica_groups=mesh['clip_0'=4,'clip_1'=8,'seq'=16] {'clip_1'}, dimensions={0}, use_global_device_ids=true | all-gather | bytes 576 | tf_op jit(solution)/shard_map/all_gather | solution.py:22
  53.9 0.6 fusion.91
  55.2 0.3 broadcast_multiply_fusion.2
  55.5 0.6 broadcast_multiply_fusion.1
  56.1 5.2 %fusion.123 = (f32[2048,64]{1,0:T(8,128)}, f32[2048,64]{1,0:T(8,128)}) fusion(f32[2048,21]{1,0:T(8,128)S(1)} %get-tuple-element.23, f32[2048,21]{1,0:T(8,128)S(1)} %get-tuple-element.22, f32[2048,22]{1,0:T(8,128)S(1)} %broadcast_multiply_fusion.2), kind=kLoop, calls=%fused_computation.132 | loop fusion | flops 262144 | bytes 1572864 | tf_op jit(solution)/shard_map/cos | solution.py:64
  61.3 33.2 %all-to-all-done = bf16[128,16,6,128]{3,0,2,1:T(8,128)(2,1)S(1)} async-done(((bf16[128,16,6,128]{3,0,2,1:T(8,128)(2,1)}), bf16[128,16,6,128]{3,0,2,1:T(8,128)(2,1)S(1)}, u32[]{:S(2)}, u32[]{:S(2)}) %all-to-all-start) | async-done | bytes 3145760 | tf_op jit(solution)/shard_map/all_to_all | solution.py:36
  94.5 0.2 copy.27
  94.7 0.0 copy-start.2
  94.7 0.1 slice_bitcast_fusion.1
  94.9 1.0 copy-done.4
  95.9 1.1 copy-done.5
  97.0 1.8 fusion.25
  98.8 0.0 copy-start
  98.8 0.6 pad_maximum_fusion.2
  99.4 0.0 copy-done.2
  99.4 0.0 copy-start.1
  99.4 1.3 fusion.81
  100.7 1.3 fusion.89
  102.0 0.0 copy-done
  102.0 0.0 copy-done.1
  102.0 4.6 %fusion = (f32[2,512]{1,0:T(2,128)S(1)}, f32[2,512,2048]{2,1,0:T(8,128)}) fusion(pred[2048]{0:T(1024)(128)(4,1)S(1)} %iota_compare_fusion, bf16[2048,2,128]{2,0,1:T(8,128)(2,1)S(1)} %pad_maximum_fusion.2, bf16[2048,2,64]{2,0,1:T(8,128)(2,1)S(1)} %get-tuple-element.12, bf16[2048,2,64]{2,0,1:T(8,128)(2,1)S(1)} %get-tuple-element.13), kind=kOutput, calls=%fused_computation.8 | convolution fusion | flops 543685632 | bytes 10491904 | tf_op jit(solution)/shard_map/qhd,khd->hqk/dot_general | solution.py:80
  106.6 10.3 %fusion.4 = (f32[2,512]{1,0:T(2,128)}, f32[2,512]{1,0:T(2,128)}, f32[2,512]{1,0:T(2,128)}, f32[2,512]{1,0:T(2,128)S(1)}, f32[2,512,2048]{2,1,0:T(8,128)}) fusion(f32[2,512,2048]{2,1,0:T(8,128)} %get-tuple-element.25, f32[2,512]{1,0:T(2,128)S(1)} %get-tuple-element.24, pred[2048]{0:T(1024)(128)(4,1)S(1)} %iota_compare_fusion, ...), kind=kOutput, calls=%fused_computation.12 | convolution fusion | flops 564654080 | bytes 35674112 | tf_op jit(solution)/shard_map/qhd,khd->hqk/dot_general | solution.py:80
  116.9 5.7 %fusion.77 = bf16[512,1,2,128]{0,3,2,1:T(8,128)(2,1)S(1)} fusion(f32[2,512,2048]{2,1,0:T(8,128)} %get-tuple-element.25, f32[2,512]{1,0:T(2,128)S(1)} %get-tuple-element.24, pred[2048]{0:T(1024)(128)(4,1)S(1)} %iota_compare_fusion, bf16[2048,1,6,128]{3,0,2,1:T(8,128)(2,1)} %bitcast.81, f32[512,2]{0,1:T(2,128)} %bitcast.92), kind=kOutput, calls=%fused_computation.68 | convolution fusion | flops 545521664 | bytes 9709568 | tf_op jit(solution)/shard_map/hqk,khd->qhd/dot_general | solution.py:97
  122.6 7.8 %fusion.6 = (f32[2,512]{1,0:T(2,128)S(1)}, f32[2,512]{1,0:T(2,128)S(1)}, f32[2,512]{1,0:T(2,128)S(1)}) fusion(f32[2,512,2048]{2,1,0:T(8,128)} %get-tuple-element.26, f32[2,512]{1,0:T(2,128)S(1)} %copy-done.8, pred[2048]{0:T(1024)(128)(4,1)S(1)} %iota_compare_fusion, f32[2,512]{1,0:T(2,128)S(1)} %copy-done.7, f32[2,512,2048]{2,1,0:T(8,128)S(1)} %fusion.81, ...), kind=kLoop, calls=%fused_computation.14 | loop fusion | flops 25162752 | bytes 25192448 | tf_op jit(solution)/shard_map/reduce_sum | solution.py:96
  130.4 5.4 %fusion.68 = bf16[512,1,2,128]{0,3,2,1:T(8,128)(2,1)S(1)} fusion(f32[2,512,2048]{2,1,0:T(8,128)} %get-tuple-element.26, f32[2,512]{1,0:T(2,128)S(1)} %copy-done.8, pred[2048]{0:T(1024)(128)(4,1)S(1)} %iota_compare_fusion, bf16[2048,1,6,128]{3,0,2,1:T(8,128)(2,1)S(1)} %bitcast.82, f32[512,2]{0,1:T(2,128)S(1)} %bitcast.91), kind=kOutput, calls=%fused_computation.65 | convolution fusion | flops 545521664 | bytes 9709568 | tf_op jit(solution)/shard_map/hqk,khd->qhd/dot_general | solution.py:97
  135.8 2.3 %fusion.59 = bf16[512,1,2,128]{0,3,2,1:T(8,128)(2,1)S(1)} fusion(f32[2,512,2048]{2,1,0:T(8,128)S(1)} %fusion.81, f32[2,512]{1,0:T(2,128)S(1)} %copy-done.7, pred[2048]{0:T(1024)(128)(4,1)S(1)} %iota_compare_fusion, bf16[2048,1,6,128]{3,0,2,1:T(8,128)(2,1)S(1)} %bitcast.83, f32[512,2]{0,1:T(2,128)S(1)} %bitcast.90), kind=kOutput, calls=%fused_computation.62 | convolution fusion | flops 545521664 | bytes 9709568 | tf_op jit(solution)/shard_map/hqk,khd->qhd/dot_general | solution.py:97
  138.2 0.0 copy-start.6
  138.2 2.4 %fusion.50 = bf16[512,1,2,128]{0,3,2,1:T(8,128)(2,1)S(1)} fusion(f32[2,512,2048]{2,1,0:T(8,128)S(1)} %fusion.89, f32[2,512]{1,0:T(2,128)S(1)} %get-tuple-element.8, pred[2048]{0:T(1024)(128)(4,1)S(1)} %iota_compare_fusion, bf16[2048,1,6,128]{3,0,2,1:T(8,128)(2,1)S(1)} %bitcast.84, f32[512,2]{0,1:T(2,128)S(1)} %bitcast.89), kind=kOutput, calls=%fused_computation.59 | convolution fusion | flops 545521664 | bytes 9709568 | tf_op jit(solution)/shard_map/hqk,khd->qhd/dot_general | solution.py:97
  140.6 0.1 pad_maximum_fusion.3
  140.7 2.0 %copy.32 = bf16[2048,1,2,128]{3,2,1,0:T(2,128)(2,1)} copy(bf16[2048,1,2,128]{0,3,2,1:T(8,128)(2,1)S(1)} %pad_maximum_fusion.3) | data formatting | bytes 2097152 | tf_op jit(solution)/shard_map/concatenate | solution.py:101
  142.7 5.4 %all-to-all-start.1 = ((bf16[2048,1,2,128]{3,2,1,0:T(2,128)(2,1)}), bf16[2048,1,2,128]{3,2,1,0:T(2,128)(2,1)S(1)}, u32[]{:S(2)}, u32[]{:S(2)}) async-start(bf16[2048,1,2,128]{3,2,1,0:T(2,128)(2,1)} %copy.32), calls=%async_computation.1 | async-start | bytes 2097152 | tf_op jit(solution)/shard_map/all_to_all | solution.py:126
  148.9 0.0 copy-done.6
  148.9 27.2 %all-to-all-done.1 = bf16[2048,1,2,128]{3,2,1,0:T(2,128)(2,1)S(1)} async-done(((bf16[2048,1,2,128]{3,2,1,0:T(2,128)(2,1)}), bf16[2048,1,2,128]{3,2,1,0:T(2,128)(2,1)S(1)}, u32[]{:S(2)}, u32[]{:S(2)}) %all-to-all-start.1) | async-done | bytes 1048608 | tf_op jit(solution)/shard_map/all_to_all | solution.py:126
  176.1 0.9 convert_bitcast_fusion
  177.0 2.6 %copy.33 = f32[128,16,1,2,128]{4,3,1,0,2:T(2,128)} copy(f32[128,16,1,2,128]{4,3,0,1,2:T(2,128)S(1)} %convert_bitcast_fusion) | data formatting | bytes 4194304 | tf_op jit(solution)/shard_map/convert_element_type | solution.py:127
  179.5 2.9 %reshape.306 = f32[1,128,4096]{2,1,0:T(8,128)S(1)} reshape(f32[128,16,1,2,128]{4,3,1,0,2:T(2,128)} %copy.33) | data formatting | bytes 4194304 | tf_op jit(solution)/shard_map/convert_element_type | solution.py:127
  182.5 1.2 select_convert_fusion
  (17 shorter events, 0.1 us)
Async XLA Ops:
  6.8 18.6 %copy-start.9 = (s32[4]{0:T(128)S(1)}, s32[4]{0:T(128)}, u32[]{:S(2)}) copy-start(s32[4]{0:T(128)} %param.10) | copy-start | bytes 52
  11.7 82.8 %all-to-all-start = ((bf16[128,16,6,128]{3,0,2,1:T(8,128)(2,1)}), bf16[128,16,6,128]{3,0,2,1:T(8,128)(2,1)S(1)}, u32[]{:S(2)}, u32[]{:S(2)}) async-start(bf16[128,16,6,128]{3,0,2,1:T(8,128)(2,1)} %copy.26), calls=%async_computation | async-start | bytes 6291456 | tf_op jit(solution)/shard_map/all_to_all | solution.py:36
  94.5 1.4 copy-start.4
  94.5 2.5 %copy-start.5 = (f32[2048,64]{1,0:T(8,128)S(1)}, f32[2048,64]{1,0:T(8,128)}, u32[]{:S(2)}) copy-start(f32[2048,64]{1,0:T(8,128)} %get-tuple-element.19) | copy-start | bytes 1572868
  94.7 4.7 %copy-start.2 = (bf16[16,128,1,6,128]{4,1,0,3,2:T(8,128)(2,1)}, bf16[16,128,1,6,128]{4,1,0,3,2:T(8,128)(2,1)S(1)}, u32[]{:S(2)}) copy-start(bf16[16,128,1,6,128]{4,1,0,3,2:T(8,128)(2,1)S(1)} %copy.27) | copy-start | bytes 9437188
  98.8 3.2 %copy-start = (bf16[2048,2,64]{2,0,1:T(8,128)(2,1)}, bf16[2048,2,64]{2,0,1:T(8,128)(2,1)S(1)}, u32[]{:S(2)}) copy-start(bf16[2048,2,64]{2,0,1:T(8,128)(2,1)S(1)} %get-tuple-element.13) | copy-start | bytes 1572868
  99.4 2.6 %copy-start.1 = (bf16[2048,2,128]{2,0,1:T(8,128)(2,1)}, bf16[2048,2,128]{2,0,1:T(8,128)(2,1)S(1)}, u32[]{:S(2)}) copy-start(bf16[2048,2,128]{2,0,1:T(8,128)(2,1)S(1)} %pad_maximum_fusion.2) | copy-start | bytes 3145732
  116.9 5.7 %copy-start.7 = (f32[2,512]{1,0:T(2,128)S(1)}, f32[2,512]{1,0:T(2,128)}, u32[]{:S(2)}) copy-start(f32[2,512]{1,0:T(2,128)} %get-tuple-element.7) | copy-start | bytes 12292
  116.9 5.7 %copy-start.8 = (f32[2,512]{1,0:T(2,128)S(1)}, f32[2,512]{1,0:T(2,128)}, u32[]{:S(2)}) copy-start(f32[2,512]{1,0:T(2,128)} %get-tuple-element.6) | copy-start | bytes 12292
  122.6 7.8 %copy-start.3 = (bf16[16,128,1,6,128]{4,1,0,3,2:T(8,128)(2,1)S(1)}, bf16[16,128,1,6,128]{4,1,0,3,2:T(8,128)(2,1)}, u32[]{:S(2)}) copy-start(bf16[16,128,1,6,128]{4,1,0,3,2:T(8,128)(2,1)} %copy-done.2) | copy-start | bytes 9437188
  138.2 10.7 %copy-start.6 = (f32[4096]{0:T(1024)S(1)}, f32[4096]{0:T(1024)}, u32[]{:S(2)}) copy-start(f32[4096]{0:T(1024)} %param.13) | copy-start | bytes 49156
  142.7 33.4 %all-to-all-start.1 = ((bf16[2048,1,2,128]{3,2,1,0:T(2,128)(2,1)}), bf16[2048,1,2,128]{3,2,1,0:T(2,128)(2,1)S(1)}, u32[]{:S(2)}, u32[]{:S(2)}) async-start(bf16[2048,1,2,128]{3,2,1,0:T(2,128)(2,1)} %copy.32), calls=%async_computation.1 | async-start | bytes 2097152 | tf_op jit(solution)/shard_map/all_to_all | solution.py:126
where the time goes:
time: 184 us
  waiting for transfers between devices  60.4 us (33%)
  matrix products  33.3 us (18%)
  blocking collectives  27.5 us (15%)
  local copies, waits for them, and re-layouts  21.2 us (12%)
  other arithmetic  21.2 us (12%)
  starting transfers between devices  17.3 us (9%)
  between operations  2.83 us (2%)
    all_to_all x1, waiting for transfers between devices, sent_together(): lax.all_to_all(both, axis, split_axis=split_dim, concat_axis=concat_dim,...  33.2 us
    all_to_all x1, waiting for transfers between devices, local(): lax.all_to_all(mixed, 'seq', split_axis=0, concat_axis=1, tiled=True)  27.2 us
    all_gather x1, blocking collectives, all_blocks(): tiles = lax.all_gather(tiles, axes[k])  20.1 us
    dot_general x4, matrix products, masked_scores(): jnp.einsum('qhd,khd->hqk', q_block, key_rot, preferred_element_type=jnp.f...  17.4 us
    dot_general x4, matrix products, attend(): jnp.einsum('hqk,khd->qhd', weights.astype(jnp.bfloat16), value, preferred...  15.8 us
    all_to_all x1, starting transfers between devices, sent_together(): lax.all_to_all(both, axis, split_axis=split_dim, concat_axis=concat_dim,...  11.8 us
    unnamed x27, local copies, waits for them, and re-layouts  10.6 us
    reduce_sum x1, other arithmetic, attend(): total = jnp.sum(weights, axis=-1)  7.78 us
  transfers between devices with their start and end apart: 2, of which 2 were waited for; matrix products, arithmetic and copies ran while one was open for 5% of the time, Pallas kernels for 0%

commit v1 on v0

--- a/solution.py
+++ b/solution.py
@@ -123,7 +123,10 @@
     key_rot = rotate(k_heads.reshape(count, heads_here, HD), cosine, sine)
     mixed = attend(query_rot, key_rot, v_heads.reshape(count, heads_here, HD), length)
     mixed = mixed.reshape(count, 1, heads_here, HD)
-    returned = lax.all_to_all(mixed, "seq", split_axis=0, concat_axis=1, tiled=True)
+    peers = lax.axis_size("seq")
+    blocks = jnp.stack(jnp.split(mixed, peers, axis=0), axis=0)
+    blocks = lax.all_to_all(blocks, "seq", split_axis=0, concat_axis=0)
+    returned = jnp.concatenate(blocks, axis=1)
     returned = returned.reshape(tok_rows, feature_count).astype(jnp.float32)
     position = lax.axis_index("seq") * tok_rows + jnp.arange(tok_rows, dtype=jnp.int32)
     gated = returned * (1.0 + sigma * gate_gain[None, :])

time: 184 us -> 184 us (level)
  local copies, waits for them, and re-layouts: 21.2 us -> 26.1 us
  other arithmetic: 21.2 us -> 17.7 us
    unnamed x27 -> x44, local copies, waits for them, and re-layouts: 10.6 us -> 20.4 us
    reduce_sum x1, other arithmetic: 7.78 us -> 3.69 us  [attend(): total = jnp.sum(weights, axis=-1)]
    convert_element_type x2 -> x1, local copies, waits for them, and re-layouts: 5.48 us -> 1.92 us  [local(): returned = returned.reshape(tok_rows, feature_count).astype(jnp.float32)]
    dot_general x4, matrix products: 15.8 us -> 12.9 us  [attend(): jnp.einsum('hqk,khd->qhd', weights.astype(jnp.bfloat16), value, preferred...]
    concatenate x1 -> x0, local copies, waits for them, and re-layouts: 2 us -> none  [attend(): return jnp.concatenate(results, axis=0).astype(jnp.bfloat16)]
where the time goes in v1:
time: 184 us; the launch traced here: 183 us
  waiting for transfers between devices  60.4 us (33%)
  matrix products  31.5 us (17%)
  blocking collectives  27.5 us (15%)
  local copies, waits for them, and re-layouts  26.1 us (14%)
  other arithmetic  17.7 us (10%)
  starting transfers between devices  17.3 us (9%)
  between operations  2.81 us (2%)
    all_to_all x1, waiting for transfers between devices, sent_together(): lax.all_to_all(both, axis, split_axis=split_dim, concat_axis=concat_dim,...  33.2 us
    all_to_all x1, waiting for transfers between devices, local(): blocks = lax.all_to_all(blocks, 'seq', split_axis=0, concat_axis=0)  27.2 us
    unnamed x44, local copies, waits for them, and re-layouts  20.4 us
    all_gather x1, blocking collectives, all_blocks(): tiles = lax.all_gather(tiles, axes[k])  20.1 us
    dot_general x4, matrix products, masked_scores(): jnp.einsum('qhd,khd->hqk', q_block, key_rot, preferred_element_type=jnp.f...  18.7 us
    dot_general x4, matrix products, attend(): jnp.einsum('hqk,khd->qhd', weights.astype(jnp.bfloat16), value, preferred...  12.9 us
    all_to_all x1, starting transfers between devices, sent_together(): lax.all_to_all(both, axis, split_axis=split_dim, concat_axis=concat_dim,...  11.8 us
    unnamed x1, blocking collectives  7.45 us
  transfers between devices with their start and end apart: 2, of which 2 were waited for; matrix products, arithmetic and copies ran while one was open for 5% of the time, Pallas kernels for 0%

profile of v1, /device:TPU:1, one launch (start us, length us, event | category | flops | bytes accessed | tf_op | source)
XLA Modules:
  0.0 183.3 jit_solution(6014155866692101332)
XLA Ops:
  0.0 2.3 %copy.22 = bf16[1,128,4096]{1,2,0:T(8,128)(2,1)} copy(bf16[1,128,4096]{2,1,0:T(8,128)(2,1)} %param.7) | data formatting | bytes 2097152 | tf_op args[0]
  2.3 2.3 %copy.23 = bf16[1,128,4096]{1,2,0:T(8,128)(2,1)} copy(bf16[1,128,4096]{2,1,0:T(8,128)(2,1)} %param.8) | data formatting | bytes 2097152 | tf_op args[1]
  4.6 2.3 %copy.24 = bf16[1,128,4096]{1,2,0:T(8,128)(2,1)} copy(bf16[1,128,4096]{2,1,0:T(8,128)(2,1)} %param.9) | data formatting | bytes 2097152 | tf_op args[2]
  6.8 2.0 %pad_maximum_fusion = bf16[128,16,6,128]{0,3,2,1:T(8,128)(2,1)S(1)} fusion(bf16[128,16,2,128]{0,3,2,1:T(8,128)(2,1)} %bitcast.133, bf16[128,16,2,128]{0,3,2,1:T(8,128)(2,1)} %bitcast.132, bf16[128,16,2,128]{0,3,2,1:T(8,128)(2,1)} %bitcast.131), kind=kLoop, calls=%fused_computation.28 | loop fusion | flops 3145728 | bytes 6291456 | tf_op jit(solution)/shard_map/concatenate | solution.py:34
  8.9 2.8 %copy.25 = bf16[128,16,6,128]{3,0,2,1:T(8,128)(2,1)} copy(bf16[128,16,6,128]{0,3,2,1:T(8,128)(2,1)S(1)} %pad_maximum_fusion) | data formatting | bytes 6291456 | tf_op jit(solution)/shard_map/concatenate | solution.py:34
  11.7 11.8 %all-to-all-start = ((bf16[128,16,6,128]{3,0,2,1:T(8,128)(2,1)}), bf16[128,16,6,128]{3,0,2,1:T(8,128)(2,1)S(1)}, u32[]{:S(2)}, u32[]{:S(2)}) async-start(bf16[128,16,6,128]{3,0,2,1:T(8,128)(2,1)} %copy.25), calls=%async_computation | async-start | bytes 6291456 | tf_op jit(solution)/shard_map/all_to_all | solution.py:36
  23.5 1.3 dynamic-slice
  25.7 7.4 %all-reduce = s32[16]{0:T(128)S(1)} all-reduce(s32[16]{0:T(128)S(1)} %dynamic-update-slice), channel_id=2, replica_groups=mesh['clip_0'=4,'clip_1'=8,'seq'=16] {'clip_0'}, use_global_device_ids=true, to_apply=%add | all-reduce | flops 16 | bytes 128
  33.9 20.1 %all-gather.2 = s32[8,4,4]{2,1,0:T(4,128)S(1)} all-gather(s32[1,4,4]{2,1,0:T(4,128)S(1)} %reshape.282), channel_id=3, replica_groups=mesh['clip_0'=4,'clip_1'=8,'seq'=16] {'clip_1'}, dimensions={0}, use_global_device_ids=true | all-gather | bytes 576 | tf_op jit(solution)/shard_map/all_gather | solution.py:22
  53.9 0.6 fusion.95
  55.2 0.3 broadcast_multiply_fusion.2
  55.5 0.6 broadcast_multiply_fusion.1
  56.1 5.2 %fusion.127 = (f32[2048,64]{1,0:T(8,128)}, f32[2048,64]{1,0:T(8,128)}) fusion(f32[2048,21]{1,0:T(8,128)S(1)} %get-tuple-element.24, f32[2048,21]{1,0:T(8,128)S(1)} %get-tuple-element.23, f32[2048,22]{1,0:T(8,128)S(1)} %broadcast_multiply_fusion.2), kind=kLoop, calls=%fused_computation.158 | loop fusion | flops 262144 | bytes 1572864 | tf_op jit(solution)/shard_map/cos | solution.py:64
  61.3 33.2 %all-to-all-done = bf16[128,16,6,128]{3,0,2,1:T(8,128)(2,1)S(1)} async-done(((bf16[128,16,6,128]{3,0,2,1:T(8,128)(2,1)}), bf16[128,16,6,128]{3,0,2,1:T(8,128)(2,1)S(1)}, u32[]{:S(2)}, u32[]{:S(2)}) %all-to-all-start) | async-done | bytes 3145760 | tf_op jit(solution)/shard_map/all_to_all | solution.py:36
  94.9 1.0 copy-done.5
  95.9 1.1 copy-done.6
  97.0 1.8 fusion.27
  98.8 0.6 pad_maximum_fusion.2
  99.4 1.3 fusion.72
  100.7 1.3 fusion.69
  102.0 5.0 %fusion.3 = (f32[2,512]{1,0:T(2,128)}, f32[2,512]{1,0:T(2,128)S(1)}, f32[2,512,2048]{2,1,0:T(8,128)}) fusion(pred[2048]{0:T(1024)(128)(4,1)S(1)} %iota_compare_fusion, f32[2,512,2048]{2,1,0:T(8,128)S(1)} %fusion.72, bf16[2048,2,128]{2,0,1:T(8,128)(2,1)S(1)} %pad_maximum_fusion.2, bf16[2048,2,64]{2,0,1:T(8,128)(2,1)S(1)} %get-tuple-element.13, ...), kind=kOutput, calls=%fused_computation.11 | convolution fusion | flops 549976064 | bytes 18884608 | tf_op jit(solution)/shard_map/qhd,khd->hqk/dot_general | solution.py:80
  107.1 11.0 %fusion.10 = (f32[2,512]{1,0:T(2,128)}, f32[2,512]{1,0:T(2,128)S(1)}, f32[2,512]{1,0:T(2,128)}, f32[2,512]{1,0:T(2,128)}, f32[2,512,2048]{2,1,0:T(8,128)}) fusion(f32[2,512,2048]{2,1,0:T(8,128)} %get-tuple-element.25, f32[2,512]{1,0:T(2,128)} %get-tuple-element.9, pred[2048]{0:T(1024)(128)(4,1)S(1)} %iota_compare_fusion, f32[2,512,2048]{2,1,0:T(8,128)S(1)} %fusion.69, ...), kind=kOutput, calls=%fused_computation.18 | convolution fusion | flops 566751232 | bytes 35678208 | tf_op jit(solution)/shard_map/qhd,khd->hqk/dot_general | solution.py:80
  118.1 5.8 %fusion.47 = bf16[512,2,128]{0,2,1:T(8,128)(2,1)S(1)} fusion(f32[2,512,2048]{2,1,0:T(8,128)} %get-tuple-element.25, f32[2,512]{1,0:T(2,128)} %get-tuple-element.9, pred[2048]{0:T(1024)(128)(4,1)S(1)} %iota_compare_fusion, bf16[2048,1,6,128]{3,0,2,1:T(8,128)(2,1)} %bitcast.126, f32[512,2]{0,1:T(2,128)} %bitcast.137), kind=kOutput, calls=%fused_computation.56 | convolution fusion | flops 545521664 | bytes 9709568 | tf_op jit(solution)/shard_map/hqk,khd->qhd/dot_general | solution.py:97
  124.2 3.7 %fusion.8 = (f32[2,512]{1,0:T(2,128)S(1)}, f32[2,512]{1,0:T(2,128)S(1)}) fusion(f32[2,512,2048]{2,1,0:T(8,128)S(1)} %fusion.69, f32[2,512]{1,0:T(2,128)S(1)} %copy-done.8, pred[2048]{0:T(1024)(128)(4,1)S(1)} %iota_compare_fusion, f32[2,512]{1,0:T(2,128)S(1)} %get-tuple-element.6, f32[2,512,2048]{2,1,0:T(8,128)S(1)} %copy-done.4), kind=kLoop, calls=%fused_computation.16 | loop fusion | flops 16775168 | bytes 16795648 | tf_op jit(solution)/shard_map/reduce_sum | solution.py:96
  127.9 2.3 %fusion.53 = bf16[512,2,128]{0,2,1:T(8,128)(2,1)S(1)} fusion(f32[2,512,2048]{2,1,0:T(8,128)S(1)} %fusion.69, f32[2,512]{1,0:T(2,128)S(1)} %copy-done.8, pred[2048]{0:T(1024)(128)(4,1)S(1)} %iota_compare_fusion, bf16[2048,1,6,128]{3,0,2,1:T(8,128)(2,1)S(1)} %bitcast.127, f32[512,2]{0,1:T(2,128)S(1)} %bitcast.135), kind=kOutput, calls=%fused_computation.58 | convolution fusion | flops 545521664 | bytes 9709568 | tf_op jit(solution)/shard_map/hqk,khd->qhd/dot_general | solution.py:97
  130.3 2.3 %fusion.59 = bf16[512,2,128]{0,2,1:T(8,128)(2,1)S(1)} fusion(f32[2,512,2048]{2,1,0:T(8,128)S(1)} %copy-done.4, f32[2,512]{1,0:T(2,128)S(1)} %get-tuple-element.6, pred[2048]{0:T(1024)(128)(4,1)S(1)} %iota_compare_fusion, bf16[2048,1,6,128]{3,0,2,1:T(8,128)(2,1)S(1)} %bitcast.128, f32[512,2]{0,1:T(2,128)S(1)} %bitcast.134), kind=kOutput, calls=%fused_computation.60 | convolution fusion | flops 545521664 | bytes 9709568 | tf_op jit(solution)/shard_map/hqk,khd->qhd/dot_general | solution.py:97
  132.6 2.4 %fusion.65 = bf16[512,2,128]{0,2,1:T(8,128)(2,1)S(1)} fusion(f32[2,512,2048]{2,1,0:T(8,128)S(1)} %fusion.72, f32[2,512]{1,0:T(2,128)S(1)} %get-tuple-element.10, pred[2048]{0:T(1024)(128)(4,1)S(1)} %iota_compare_fusion, bf16[2048,1,6,128]{3,0,2,1:T(8,128)(2,1)S(1)} %bitcast.129, f32[512,2]{0,1:T(2,128)S(1)} %bitcast.136), kind=kOutput, calls=%fused_computation.62 | convolution fusion | flops 545521664 | bytes 9709568 | tf_op jit(solution)/shard_map/hqk,khd->qhd/dot_general | solution.py:97
  135.0 0.6 fusion.94
  135.6 0.6 fusion.93
  136.3 0.6 fusion.92
  136.9 0.6 fusion.91
  137.5 0.6 fusion.90
  138.2 0.6 fusion.89
  138.8 0.6 fusion.88
  139.4 0.6 fusion.87
  140.1 0.6 fusion.86
  140.7 0.6 fusion.85
  141.4 0.6 fusion.84
  142.0 0.6 fusion.83
  142.6 0.6 fusion.82
  143.3 0.6 fusion.81
  143.9 0.6 fusion.80
  144.6 0.6 fusion.79
  145.2 5.4 %all-to-all-start.1 = ((bf16[16,128,1,2,128]{1,4,3,2,0:T(8,128)(2,1)}), bf16[16,128,1,2,128]{1,4,3,2,0:T(8,128)(2,1)S(1)}, u32[]{:S(2)}, u32[]{:S(2)}) async-start(bf16[16,128,1,2,128]{1,4,3,2,0:T(8,128)(2,1)} %fusion.79), calls=%async_computation.1 | async-start | bytes 2097152 | tf_op jit(solution)/shard_map/all_to_all | solution.py:128
  151.4 27.2 %all-to-all-done.1 = bf16[16,128,1,2,128]{1,4,3,2,0:T(8,128)(2,1)S(1)} async-done(((bf16[16,128,1,2,128]{1,4,3,2,0:T(8,128)(2,1)}), bf16[16,128,1,2,128]{1,4,3,2,0:T(8,128)(2,1)S(1)}, u32[]{:S(2)}, u32[]{:S(2)}) %all-to-all-start.1) | async-done | bytes 1048608 | tf_op jit(solution)/shard_map/all_to_all | solution.py:128
  178.6 1.6 convert_element_type.95
  180.2 1.9 %copy.31 = f32[1,128,4096]{2,1,0:T(8,128)S(1)} copy(f32[1,128,4096]{1,2,0:T(8,128)} %bitcast.130) | data formatting | bytes 4194304 | tf_op jit(solution)/shard_map/convert_element_type | solution.py:130
  182.1 1.2 select_convert_fusion
  (32 shorter events, 1.0 us)
Async XLA Ops:
  6.8 18.6 %copy-start.9 = (s32[4]{0:T(128)S(1)}, s32[4]{0:T(128)}, u32[]{:S(2)}) copy-start(s32[4]{0:T(128)} %param.10) | copy-start | bytes 52
  11.7 82.8 %all-to-all-start = ((bf16[128,16,6,128]{3,0,2,1:T(8,128)(2,1)}), bf16[128,16,6,128]{3,0,2,1:T(8,128)(2,1)S(1)}, u32[]{:S(2)}, u32[]{:S(2)}) async-start(bf16[128,16,6,128]{3,0,2,1:T(8,128)(2,1)} %copy.25), calls=%async_computation | async-start | bytes 6291456 | tf_op jit(solution)/shard_map/all_to_all | solution.py:36
  94.5 1.4 copy-start.5
  94.5 2.5 %copy-start.6 = (f32[2048,64]{1,0:T(8,128)S(1)}, f32[2048,64]{1,0:T(8,128)}, u32[]{:S(2)}) copy-start(f32[2048,64]{1,0:T(8,128)} %get-tuple-element.20) | copy-start | bytes 1572868
  94.7 4.7 %copy-start.2 = (bf16[16,128,1,6,128]{4,1,0,3,2:T(8,128)(2,1)}, bf16[16,128,1,6,128]{4,1,0,3,2:T(8,128)(2,1)S(1)}, u32[]{:S(2)}) copy-start(bf16[16,128,1,6,128]{4,1,0,3,2:T(8,128)(2,1)S(1)} %copy.26) | copy-start | bytes 9437188
  98.8 3.2 %copy-start = (bf16[2048,2,64]{2,0,1:T(8,128)(2,1)}, bf16[2048,2,64]{2,0,1:T(8,128)(2,1)S(1)}, u32[]{:S(2)}) copy-start(bf16[2048,2,64]{2,0,1:T(8,128)(2,1)S(1)} %get-tuple-element.14) | copy-start | bytes 1572868
  99.4 2.6 %copy-start.1 = (bf16[2048,2,128]{2,0,1:T(8,128)(2,1)}, bf16[2048,2,128]{2,0,1:T(8,128)(2,1)S(1)}, u32[]{:S(2)}) copy-start(bf16[2048,2,128]{2,0,1:T(8,128)(2,1)S(1)} %pad_maximum_fusion.2) | copy-start | bytes 3145732
  118.1 6.1 %copy-start.4 = (f32[2,512,2048]{2,1,0:T(8,128)S(1)}, f32[2,512,2048]{2,1,0:T(8,128)}, u32[]{:S(2)}) copy-start(f32[2,512,2048]{2,1,0:T(8,128)} %get-tuple-element.26) | copy-start | bytes 25165828
  118.1 6.1 %copy-start.8 = (f32[2,512]{1,0:T(2,128)S(1)}, f32[2,512]{1,0:T(2,128)}, u32[]{:S(2)}) copy-start(f32[2,512]{1,0:T(2,128)} %get-tuple-element.7) | copy-start | bytes 12292
  124.2 3.7 %copy-start.3 = (bf16[16,128,1,6,128]{4,1,0,3,2:T(8,128)(2,1)S(1)}, bf16[16,128,1,6,128]{4,1,0,3,2:T(8,128)(2,1)}, u32[]{:S(2)}) copy-start(bf16[16,128,1,6,128]{4,1,0,3,2:T(8,128)(2,1)} %copy-done.2) | copy-start | bytes 9437188
  130.2 2.4 %copy-start.10 = (f32[2,512]{1,0:T(2,128)S(1)}, f32[2,512]{1,0:T(2,128)}, u32[]{:S(2)}) copy-start(f32[2,512]{1,0:T(2,128)} %get-tuple-element.8) | copy-start | bytes 12292
  132.6 18.7 %copy-start.7 = (f32[4096]{0:T(1024)S(1)}, f32[4096]{0:T(1024)}, u32[]{:S(2)}) copy-start(f32[4096]{0:T(1024)} %param.13) | copy-start | bytes 49156
  145.2 33.4 %all-to-all-start.1 = ((bf16[16,128,1,2,128]{1,4,3,2,0:T(8,128)(2,1)}), bf16[16,128,1,2,128]{1,4,3,2,0:T(8,128)(2,1)S(1)}, u32[]{:S(2)}, u32[]{:S(2)}) async-start(bf16[16,128,1,2,128]{1,4,3,2,0:T(8,128)(2,1)} %fusion.79), calls=%async_computation.1 | async-start | bytes 2097152 | tf_op jit(solution)/shard_map/all_to_all | solution.py:128
